TPU v7x, 256 devices: a whole 4x4x8 slice. The times are simulated.
256 devices in a mesh: light: 64 (over y, x_lo, z), tex: 4 (over x_hi, core).
Axes of the slice: x: 4 (x_hi: 2, x_lo: 2; x = x_hi * 2 + x_lo), y: 4, z: 8, core: 2. Of those that a mesh axis runs over, the one named last changes fastest.
Arguments:
- light_ids: int32 [128], P('light'), may hold values from 0 to 255
- tile_offsets: int32 [128], P('light'), may hold values from 0 to 4095
- light_table: bfloat16 [256, 512], replicated, may hold values from -6 to 6
- hyper_weight: bfloat16 [512, 1179648], P(None, ('light', 'tex')), may hold values from -0.25 to 0.25
- features: bfloat16 [128, 64, 48, 256], P('light', 'tex'), may hold values from -6 to 6
- upstream_grad: bfloat16 [128, 64, 48, 256], P('light', 'tex'), may hold values from -3 to 3
Outputs:
- relit: bfloat16 [128, 64, 48, 256], P('light', 'tex')
- feature_grad: bfloat16 [128, 64, 48, 256], P('light', 'tex')
- hyper_grad: bfloat16 [512, 1179648], P(None, ('light', 'tex'))
All inputs are finite; a program needn't handle non-finite values.
Results may differ from a plain program's by a relative error of at most 0.02.
Values may be sent and summed in bfloat16 or wider, within the bound.
A program may use at most 128 MiB of HBM per device.

v0:
```python
import math
import jax
import jax.numpy as jnp
from jax import lax
from jax.sharding import PartitionSpec as P


def padded_2(block, sides, width):
    for axis, dim in sides:
        count = lax.axis_size(axis)
        forward = [(i, i + 1) for i in range(count - 1)]
        backward = [(target, source) for source, target in forward]
        low = lax.ppermute(
            lax.slice_in_dim(block, block.shape[dim] - width, None, axis=dim), axis, forward
        )
        high = lax.ppermute(lax.slice_in_dim(block, 0, width, axis=dim), axis, backward)
        block = jnp.concatenate([low, block, high], axis=dim)
    return block


def smooth_act(values):
    return values * jax.nn.sigmoid(values)


def smooth_slope(values):
    sig = jax.nn.sigmoid(values)
    return sig * (1.0 + values * (1.0 - sig))


def light_codes(light_ids, tile_offsets, light_table):
    halfway = light_table.shape[1] // 2
    onehot = (
        light_ids[:, None] == jnp.arange(light_table.shape[0], dtype=jnp.int32)[None, :]
    ).astype(jnp.bfloat16)
    looked = jnp.dot(onehot, light_table, preferred_element_type=jnp.float32)
    rates = jnp.exp(-math.log(1000.0) * jnp.arange(halfway, dtype=jnp.float32) / halfway)
    angles = tile_offsets.astype(jnp.float32)[:, None] * rates[None, :]
    summed = looked + jnp.concatenate([jnp.sin(angles), jnp.cos(angles)], axis=1)
    return (summed * lax.rsqrt(jnp.mean(summed * summed, axis=1, keepdims=True) + 1e-06)).astype(
        jnp.bfloat16
    )


def build_patches(padded, out_rows):
    columns = padded.shape[2]
    wide = jnp.pad(padded, ((0, 0), (0, 0), (1, 1), (0, 0)))
    pieces = [
        wide[:, row_tap : row_tap + out_rows, col_tap : col_tap + columns, :]
        for row_tap in range(3)
        for col_tap in range(3)
    ]
    return jnp.concatenate(pieces, axis=3)


def apply_conv(patches, kernel):
    return jnp.einsum("lrck,lko->lrco", patches, kernel, preferred_element_type=jnp.float32)


def kernel_grad(patches, upstream):
    return jnp.einsum("lrck,lrco->lko", patches, upstream, preferred_element_type=jnp.float32)


def flipped(kernel):
    lights_here, depth, channels = kernel.shape
    shaped = kernel.reshape(lights_here, 3, 3, channels, channels)
    return shaped[:, ::-1, ::-1].swapaxes(3, 4).reshape(lights_here, depth, channels)


def shards(light_ids, tile_offsets, light_table, hyper_weight, features, upstream_grad):
    lights_dev, rows_dev, channels = (features.shape[0], features.shape[1], features.shape[3])
    scale = 1.0 / math.sqrt(9 * channels)
    kernel_len = 9 * channels * channels
    own_codes = light_codes(light_ids, tile_offsets, light_table)
    all_codes = lax.all_gather(own_codes, "light", axis=0, tiled=True)
    columns = (scale * jnp.dot(all_codes, hyper_weight, preferred_element_type=jnp.float32)).astype(
        jnp.bfloat16
    )
    quarters = lax.all_gather(columns, "tex", axis=1, tiled=True)
    weights = lax.all_to_all(quarters, "light", split_axis=0, concat_axis=1, tiled=True)
    first_kernel = weights[:, :kernel_len].reshape(lights_dev, 9 * channels, channels)
    second_kernel = weights[:, kernel_len:].reshape(lights_dev, 9 * channels, channels)
    padded_in = padded_2(features, (("tex", 1),), 1)
    input_patches = build_patches(padded_in, rows_dev)
    first_pre = apply_conv(input_patches, first_kernel)
    hidden = smooth_act(first_pre).astype(jnp.bfloat16)
    padded_hidden = padded_2(hidden, (("tex", 1),), 1)
    hidden_patches = build_patches(padded_hidden, rows_dev)
    second_pre = apply_conv(hidden_patches, second_kernel)
    relit = smooth_act(second_pre).astype(jnp.bfloat16)
    second_grad = (upstream_grad * smooth_slope(second_pre)).astype(jnp.bfloat16)
    padded_grad = padded_2(second_grad, (("tex", 1),), 1)
    hidden_grad = apply_conv(build_patches(padded_grad, rows_dev), flipped(second_kernel))
    first_grad = (hidden_grad * smooth_slope(first_pre)).astype(jnp.bfloat16)
    padded_first = padded_2(first_grad, (("tex", 1),), 1)
    feature_grad = apply_conv(build_patches(padded_first, rows_dev), flipped(first_kernel)).astype(
        jnp.bfloat16
    )
    first_kgrad = kernel_grad(input_patches, first_grad)
    second_kgrad = kernel_grad(hidden_patches, second_grad)
    grads = jnp.concatenate(
        [first_kgrad.reshape(lights_dev, -1), second_kgrad.reshape(lights_dev, -1)], axis=1
    )
    spread = lax.all_to_all(
        grads.astype(jnp.bfloat16), "light", split_axis=1, concat_axis=0, tiled=True
    ).astype(grads.dtype)
    summed = lax.psum_scatter(spread.astype(jnp.bfloat16), "tex", scatter_dimension=1, tiled=True)
    hyper_grad = (
        scale * jnp.einsum("lz,ls->zs", all_codes, summed, preferred_element_type=jnp.float32)
    ).astype(jnp.bfloat16)
    return (relit, feature_grad, hyper_grad)


def solution(mesh):
    in_specs = (
        P("light"),
        P("light"),
        P(),
        P(None, ("light", "tex")),
        P("light", "tex", None, None),
        P("light", "tex", None, None),
    )
    out_specs = (
        P("light", "tex", None, None),
        P("light", "tex", None, None),
        P(None, ("light", "tex")),
    )
    return jax.shard_map(shards, mesh=mesh, in_specs=in_specs, out_specs=out_specs, check_vma=False)
```

profile of v0, /device:TPU:1, one launch (start us, length us, event | category | flops | bytes accessed | tf_op | source)
XLA Modules:
  0.0 607.9 jit_solution(14286666769212236578)
XLA Ops:
  8.1 1.0 multiply_reduce_fusion
  9.2 132.7 %all-gather = bf16[64,2,512]{2,1,0:T(2,128)(2,1)S(1)} all-gather(bf16[1,2,512]{2,1,0:T(2,128)(2,1)S(1)} %fusion.21), channel_id=1, replica_groups=mesh['light'=64,'tex'=4] {'light'}, dimensions={0}, use_global_device_ids=true | all-gather | bytes 133120 | tf_op jit(solution)/shard_map/all_gather | solution.py:74
  141.9 4.1 fusion
  146.1 65.8 %all-gather.3.cloned.1.call-done = bf16[128,18432]{1,0:T(8,128)(2,1)} async-done(((bf16[128,4608]{1,0:T(8,128)(2,1)}), bf16[128,18432]{1,0:T(8,128)(2,1)}) %all-gather.3.cloned.1.call-update) | async-done | bytes 4718608 | tf_op jit(solution)/shard_map/all_gather | solution.py:78
  212.0 7.9 %all_to_all.26 = bf16[64,2,18432]{2,1,0:T(2,128)(2,1)} reshape(bf16[128,18432]{1,0:T(8,128)(2,1)} %all-gather.3.cloned.1.call-done) | data formatting | bytes 9437184 | tf_op jit(solution)/shard_map/all_to_all | solution.py:79
  219.9 10.6 %all-to-all-start = ((bf16[64,2,18432]{2,1,0:T(2,128)(2,1)}), bf16[64,2,18432]{2,1,0:T(2,128)(2,1)}, u32[]{:S(2)}, u32[]{:S(2)}) async-start(bf16[64,2,18432]{2,1,0:T(2,128)(2,1)} %all_to_all.26), calls=%async_computation | async-start | bytes 9437184 | tf_op jit(solution)/shard_map/all_to_all | solution.py:79
  230.5 4.1 collective-permute-start
  234.7 1.9 collective-permute-start.1
  236.6 4.8 collective-permute-done
  241.4 3.0 collective-permute-done.1
  245.0 1.0 slice_dynamic-update-slice_fusion.23
  246.1 1.1 fusion.18
  247.1 1.3 slice_dynamic-update-slice_fusion.22
  248.4 1.0 slice_dynamic-update-slice_fusion.21
  249.4 1.0 constant_dynamic-update-slice_fusion
  250.4 1.4 slice_dynamic-update-slice_fusion.20
  251.8 1.0 slice_dynamic-update-slice_fusion.19
  252.7 1.0 fusion.17
  253.8 1.3 slice_dynamic-update-slice_fusion.18
  255.1 77.5 %all-to-all-done = bf16[64,2,18432]{2,1,0:T(2,128)(2,1)} async-done(((bf16[64,2,18432]{2,1,0:T(2,128)(2,1)}), bf16[64,2,18432]{2,1,0:T(2,128)(2,1)}, u32[]{:S(2)}, u32[]{:S(2)}) %all-to-all-start) | async-done | bytes 4718624 | tf_op jit(solution)/shard_map/all_to_all | solution.py:79
  332.6 5.5 fusion.25
  338.1 8.0 %multiply_convert_fusion.4 = (bf16[2,16,48,256]{3,2,1,0:T(8,128)(2,1)S(1)}, f32[2,16,48,256]{3,2,1,0:T(8,128)}) fusion(bf16[2,16,48,2304]{3,2,1,0:T(8,128)(2,1)} %slice_dynamic-update-slice_fusion.18, bf16[1,2,2304,256]{3,1,2,0:T(2,128)(2,1)S(1)} %bitcast.80), kind=kOutput, calls=%fused_computation.19 | convolution fusion | flops 1813905408 | bytes 11796480 | tf_op jit(solution)/shard_map/lrck,lko->lrco/dot_general | solution.py:56
  346.2 10.2 %collective-permute-start.2 = (bf16[2,1,48,256]{3,2,1,0:T(8,128)(2,1)S(1)}, bf16[2,1,48,256]{3,2,1,0:T(8,128)(2,1)S(1)}, u32[]{:S(2)}, u32[]{:S(2)}) collective-permute-start(bf16[2,1,48,256]{3,2,1,0:T(8,128)(2,1)S(1)} %get-tuple-element.11), channel_id=1, source_target_pairs={{0,1},{1,2},{2,3},{4,5},{5,6},{6,7},{8,9},{9,10},{10,11},{12,13},{... | collective-permute-start | bytes 147464 | tf_op jit(solution)/shard_map/ppermute | solution.py:13
  356.4 2.2 collective-permute-start.3
  358.6 1.7 copy.26
  360.3 2.8 copy.15
  363.2 1.6 rev.6
  367.7 3.4 multiply_convert_fusion.2
  371.1 5.1 collective-permute-start.4
  376.3 1.9 collective-permute-start.5
  378.2 4.4 fusion.2
  382.6 3.5 concatenate.78
  386.2 3.8 copy.18
  393.2 2.3 multiply_convert_fusion.1
  395.5 7.3 %fusion.1 = bf16[2,2304,256]{2,1,0:T(8,128)(2,1)} fusion(bf16[2,16,48,2304]{3,2,1,0:T(8,128)(2,1)} %slice_dynamic-update-slice_fusion.18, bf16[2,16,48,256]{3,2,1,0:T(8,128)(2,1)S(1)} %multiply_convert_fusion.1), kind=kOutput, calls=%fused_computation.6 | convolution fusion | flops 1813118976 | bytes 10223616 | tf_op jit(solution)/shard_map/lrck,lrco->lko/dot_general | solution.py:60
  402.8 3.2 concatenate.77
  406.0 3.9 copy.17
  409.8 10.6 %pad_maximum_fusion = bf16[2,64,18432]{2,0,1:T(2,128)(2,1)} fusion(bf16[2,32,18432]{2,0,1:T(2,128)(2,1)} %copy.18, bf16[2,32,18432]{2,0,1:T(2,128)(2,1)} %copy.17), kind=kLoop, calls=%fused_computation.5 | loop fusion | flops 2359296 | bytes 9437184 | tf_op jit(solution)/shard_map/concatenate | solution.py:100
  420.4 111.9 %all_to_all.35 = bf16[2,64,18432]{2,0,1:T(2,128)(2,1)} all-to-all(bf16[2,64,18432]{2,0,1:T(2,128)(2,1)} %pad_maximum_fusion), channel_id=1, replica_groups=mesh['light'=64,'tex'=4] {'light'}, dimensions={1} | all-to-all | bytes 9437184 | tf_op jit(solution)/shard_map/all_to_all | solution.py:103
  532.3 7.5 %all_to_all.32 = bf16[128,18432]{1,0:T(8,128)(2,1)} reshape(bf16[64,2,18432]{2,1,0:T(2,128)(2,1)} %bitcast.77) | data formatting | bytes 9437184 | tf_op jit(solution)/shard_map/all_to_all | solution.py:103
  539.9 5.4 collective-permute-start.6
  545.3 1.9 collective-permute-start.7
  547.2 2.0 copy.25
  549.2 2.7 copy.16
  551.9 2.0 rev.7
  556.0 2.9 convolution_convert_fusion
  558.9 37.0 %reduce-scatter.2.cloned.1.call-done = bf16[128,4608]{1,0:T(8,128)(2,1)} async-done(((bf16[128,18432]{1,0:T(8,128)(2,1)}), bf16[128,4608]{1,0:T(8,128)(2,1)}) %reduce-scatter.2.cloned.1.call-update) | async-done | bytes 1179664 | tf_op jit(solution)/shard_map/reduce_scatter | solution.py:106
  596.0 4.9 multiply_convert_fusion
  (69 shorter events, 9.8 us)
Async XLA Ops:
  7.2 1.0 copy-start
  7.2 204.8 %all-gather.3.cloned.1.call-start = ((), (), s32[]{:S(2)}) async-start(), calls=%async_computation.3 | async-start | bytes 5898240 | tf_op jit(solution)/shard_map/all_gather | solution.py:78
  219.9 10.6 %copy-start.2 = (bf16[2,16,48,256]{3,2,1,0:T(8,128)(2,1)S(1)}, bf16[2,16,48,256]{3,2,1,0:T(8,128)(2,1)}, u32[]{:S(2)}) copy-start(bf16[2,16,48,256]{3,2,1,0:T(8,128)(2,1)} %param.10) | copy-start | bytes 2359300
  219.9 112.7 %all-to-all-start = ((bf16[64,2,18432]{2,1,0:T(2,128)(2,1)}), bf16[64,2,18432]{2,1,0:T(2,128)(2,1)}, u32[]{:S(2)}, u32[]{:S(2)}) async-start(bf16[64,2,18432]{2,1,0:T(2,128)(2,1)} %all_to_all.26), calls=%async_computation | async-start | bytes 9437184 | tf_op jit(solution)/shard_map/all_to_all | solution.py:79
  230.5 365.5 %reduce-scatter.2.cloned.1.call-start = ((), (), s32[]{:S(2)}) async-start(), calls=%async_computation.4 | async-start | bytes 5898240 | tf_op jit(solution)/shard_map/reduce_scatter | solution.py:106
  230.5 10.9 %collective-permute-start = (bf16[2,1,48,256]{3,2,1,0:T(8,128)(2,1)S(1)}, bf16[2,1,48,256]{3,2,1,0:T(8,128)(2,1)S(1)}, u32[]{:S(2)}, u32[]{:S(2)}) collective-permute-start(bf16[2,1,48,256]{3,2,1,0:T(8,128)(2,1)S(1)} %get-tuple-element.13), channel_id=1, source_target_pairs={{0,1},{1,2},{2,3},{4,5},{5,6},{6,7},{8,9},{9,10},{10,11},{12,13},{... | collective-permute-start | bytes 147464 | tf_op jit(solution)/shard_map/ppermute | solution.py:13
  234.7 9.8 %collective-permute-start.1 = (bf16[2,1,48,256]{3,2,1,0:T(8,128)(2,1)S(1)}, bf16[2,1,48,256]{3,2,1,0:T(8,128)(2,1)S(1)}, u32[]{:S(2)}, u32[]{:S(2)}) collective-permute-start(bf16[2,1,48,256]{3,2,1,0:T(8,128)(2,1)S(1)} %get-tuple-element.14), channel_id=1, source_target_pairs={{1,0},{2,1},{3,2},{5,4},{6,5},{7,6},{9,8},{10,9},{11,10},{13,12},{... | collective-permute-start | bytes 147464 | tf_op jit(solution)/shard_map/ppermute | solution.py:16
  338.1 8.0 %copy-start.3 = (bf16[2,589824]{1,0:T(2,128)(2,1)}, bf16[2,589824]{1,0:T(2,128)(2,1)S(1)}, u32[]{:S(2)}) copy-start(bf16[2,589824]{1,0:T(2,128)(2,1)S(1)} %get-tuple-element.4) | copy-start | bytes 7077892
  338.1 20.5 %copy-start.4 = (bf16[2,589824]{1,0:T(2,128)(2,1)}, bf16[2,589824]{1,0:T(2,128)(2,1)S(1)}, u32[]{:S(2)}) copy-start(bf16[2,589824]{1,0:T(2,128)(2,1)S(1)} %get-tuple-element.3) | copy-start | bytes 7077892
  346.2 18.6 %collective-permute-start.2 = (bf16[2,1,48,256]{3,2,1,0:T(8,128)(2,1)S(1)}, bf16[2,1,48,256]{3,2,1,0:T(8,128)(2,1)S(1)}, u32[]{:S(2)}, u32[]{:S(2)}) collective-permute-start(bf16[2,1,48,256]{3,2,1,0:T(8,128)(2,1)S(1)} %get-tuple-element.11), channel_id=1, source_target_pairs={{0,1},{1,2},{2,3},{4,5},{5,6},{6,7},{8,9},{9,10},{10,11},{12,13},{... | collective-permute-start | bytes 147464 | tf_op jit(solution)/shard_map/ppermute | solution.py:13
  356.4 8.4 %collective-permute-start.3 = (bf16[2,1,48,256]{3,2,1,0:T(8,128)(2,1)S(1)}, bf16[2,1,48,256]{3,2,1,0:T(8,128)(2,1)S(1)}, u32[]{:S(2)}, u32[]{:S(2)}) collective-permute-start(bf16[2,1,48,256]{3,2,1,0:T(8,128)(2,1)S(1)} %get-tuple-element.12), channel_id=1, source_target_pairs={{1,0},{2,1},{3,2},{5,4},{6,5},{7,6},{9,8},{10,9},{11,10},{13,12},{... | collective-permute-start | bytes 147464 | tf_op jit(solution)/shard_map/ppermute | solution.py:16
  365.9 1.7 copy-start.5
  365.9 1.8 copy-start.7
  371.1 18.8 %collective-permute-start.4 = (bf16[2,1,48,256]{3,2,1,0:T(8,128)(2,1)S(1)}, bf16[2,1,48,256]{3,2,1,0:T(8,128)(2,1)S(1)}, u32[]{:S(2)}, u32[]{:S(2)}) collective-permute-start(bf16[2,1,48,256]{3,2,1,0:T(8,128)(2,1)S(1)} %get-tuple-element.9), channel_id=1, source_target_pairs={{0,1},{1,2},{2,3},{4,5},{5,6},{6,7},{8,9},{9,10},{10,11},{12,13},{... | collective-permute-start | bytes 147464 | tf_op jit(solution)/shard_map/ppermute | solution.py:13
  376.3 13.7 %collective-permute-start.5 = (bf16[2,1,48,256]{3,2,1,0:T(8,128)(2,1)S(1)}, bf16[2,1,48,256]{3,2,1,0:T(8,128)(2,1)S(1)}, u32[]{:S(2)}, u32[]{:S(2)}) collective-permute-start(bf16[2,1,48,256]{3,2,1,0:T(8,128)(2,1)S(1)} %get-tuple-element.10), channel_id=1, source_target_pairs={{1,0},{2,1},{3,2},{5,4},{6,5},{7,6},{9,8},{10,9},{11,10},{13,12},{... | collective-permute-start | bytes 147464 | tf_op jit(solution)/shard_map/ppermute | solution.py:16
  391.1 1.7 copy-start.6
  391.1 2.1 copy-start.8
  539.9 14.0 %collective-permute-start.6 = (bf16[2,1,48,256]{3,2,1,0:T(8,128)(2,1)S(1)}, bf16[2,1,48,256]{3,2,1,0:T(8,128)(2,1)S(1)}, u32[]{:S(2)}, u32[]{:S(2)}) collective-permute-start(bf16[2,1,48,256]{3,2,1,0:T(8,128)(2,1)S(1)} %get-tuple-element.7), channel_id=1, source_target_pairs={{0,1},{1,2},{2,3},{4,5},{5,6},{6,7},{8,9},{9,10},{10,11},{12,13},{... | collective-permute-start | bytes 147464 | tf_op jit(solution)/shard_map/ppermute | solution.py:13
  545.3 8.6 %collective-permute-start.7 = (bf16[2,1,48,256]{3,2,1,0:T(8,128)(2,1)S(1)}, bf16[2,1,48,256]{3,2,1,0:T(8,128)(2,1)S(1)}, u32[]{:S(2)}, u32[]{:S(2)}) collective-permute-start(bf16[2,1,48,256]{3,2,1,0:T(8,128)(2,1)S(1)} %get-tuple-element.8), channel_id=1, source_target_pairs={{1,0},{2,1},{3,2},{5,4},{6,5},{7,6},{9,8},{10,9},{11,10},{13,12},{... | collective-permute-start | bytes 147464 | tf_op jit(solution)/shard_map/ppermute | solution.py:16
  556.0 44.8 %copy-start.1 = (bf16[256,512]{1,0:T(8,128)(2,1)S(1)}, bf16[256,512]{1,0:T(8,128)(2,1)}, u32[]{:S(2)}) copy-start(bf16[256,512]{1,0:T(8,128)(2,1)} %param.8) | copy-start | bytes 786436
Sparse Core Ops, SparseCore 0:
  146.2 65.6 all-gather.2
  540.0 55.9 reduce-scatter.1
where the time goes:
time: 615 us; the launch traced here: 608 us
  blocking collectives  245 us (40%)
  waiting for transfers between devices  188 us (31%)
  local copies, waits for them, and re-layouts  62.3 us (10%)
  starting transfers between devices  43.5 us (7%)
  matrix products  38.3 us (6%)
  other arithmetic  16.2 us (3%)
  between operations  14.7 us (2%)
    all_gather x1, blocking collectives, shards(): all_codes = lax.all_gather(own_codes, 'light', axis=0, tiled=True)  133 us
    all_to_all x1, blocking collectives, shards(): lax.all_to_all(grads.astype(jnp.bfloat16), 'light', split_axis=1, concat_...  112 us
    all_to_all x1, waiting for transfers between devices, shards(): lax.all_to_all(quarters, 'light', split_axis=0, concat_axis=1, tiled=True)  77.5 us
    all_gather x1, waiting for transfers between devices, shards(): quarters = lax.all_gather(columns, 'tex', axis=1, tiled=True)  65.8 us
    reduce_scatter x1, waiting for transfers between devices, shards(): lax.psum_scatter(spread.astype(jnp.bfloat16), 'tex', scatter_dimension=1,...  37 us
    ppermute x4, starting transfers between devices, padded_2(): lax.ppermute(lax.slice_in_dim(block, block.shape[dim] - width, None, axis...  24.9 us
    dot_general x4, matrix products, apply_conv(): jnp.einsum('lrck,lko->lrco', patches, kernel, preferred_element_type=jnp....  16.6 us
    unnamed x45, local copies, waits for them, and re-layouts  15.4 us
  transfers between devices with their start and end apart: 11, of which 5 were waited for; matrix products, arithmetic and copies ran while one was open for 7% of the time, Pallas kernels for 0%

commit v1 on v0

--- a/solution.py
+++ b/solution.py
@@ -75,7 +75,9 @@
     columns = (scale * jnp.dot(all_codes, hyper_weight, preferred_element_type=jnp.float32)).astype(
         jnp.bfloat16
     )
-    quarters = lax.all_gather(columns, "tex", axis=1, tiled=True)
+    quarters = jnp.concatenate(
+        lax.all_to_all(jnp.stack([columns for _ in range(lax.axis_size("tex"))], 0), "tex", 0, 0), 1
+    )
     weights = lax.all_to_all(quarters, "light", split_axis=0, concat_axis=1, tiled=True)
     first_kernel = weights[:, :kernel_len].reshape(lights_dev, 9 * channels, channels)
     second_kernel = weights[:, kernel_len:].reshape(lights_dev, 9 * channels, channels)

time: 615 us -> 638 us (1.037)
  blocking collectives: 245 us -> 331 us
  waiting for transfers between devices: 188 us -> 123 us
  local copies, waits for them, and re-layouts: 62.3 us -> 72.1 us
  starting transfers between devices: 43.5 us -> 36.4 us
    all_to_all x0 -> x1, blocking collectives: none -> 86.7 us  [shards(): lax.all_to_all(jnp.stack([columns for _ in range(lax.axis_size('tex'))],...]
    all_gather x1 -> x0, waiting for transfers between devices: 65.8 us -> none  [shards(): quarters = lax.all_gather(columns, 'tex', axis=1, tiled=True)]
  transfers between devices with their start and end apart: 11 -> 10, of which waited for: 5 -> 4; matrix products, arithmetic and copies ran while one was open for 7% -> 6% of each run, Pallas kernels for 0% -> 0%
where the time goes in v1:
time: 638 us; the launch traced here: 631 us
  blocking collectives  331 us (52%)
  waiting for transfers between devices  123 us (19%)
  local copies, waits for them, and re-layouts  72.1 us (11%)
  matrix products  37.2 us (6%)
  starting transfers between devices  36.4 us (6%)
  other arithmetic  16.2 us (3%)
  between operations  14.8 us (2%)
    all_gather x1, blocking collectives, shards(): all_codes = lax.all_gather(own_codes, 'light', axis=0, tiled=True)  133 us
    all_to_all x1, blocking collectives, shards(): lax.all_to_all(grads.astype(jnp.bfloat16), 'light', split_axis=1, concat_...  112 us
    all_to_all x1, blocking collectives, shards(): lax.all_to_all(jnp.stack([columns for _ in range(lax.axis_size('tex'))],...  86.7 us
    all_to_all x1, waiting for transfers between devices, shards(): lax.all_to_all(quarters, 'light', split_axis=0, concat_axis=1, tiled=True)  78.8 us
    reduce_scatter x1, waiting for transfers between devices, shards(): lax.psum_scatter(spread.astype(jnp.bfloat16), 'tex', scatter_dimension=1,...  37 us
    ppermute x4, starting transfers between devices, padded_2(): lax.ppermute(lax.slice_in_dim(block, block.shape[dim] - width, None, axis...  22.3 us
    dot_general x4, matrix products, apply_conv(): jnp.einsum('lrck,lko->lrco', patches, kernel, preferred_element_type=jnp....  16.6 us
    unnamed x45, local copies, waits for them, and re-layouts  15.5 us
  transfers between devices with their start and end apart: 10, of which 4 were waited for; matrix products, arithmetic and copies ran while one was open for 6% of the time, Pallas kernels for 0%

profile of v1, /device:TPU:1, one launch (start us, length us, event | category | flops | bytes accessed | tf_op | source)
XLA Modules:
  0.0 631.2 jit_solution(14141263639598180708)
XLA Ops:
  9.2 132.7 %all-gather = bf16[64,2,512]{2,1,0:T(2,128)(2,1)S(1)} all-gather(bf16[1,2,512]{2,1,0:T(2,128)(2,1)S(1)} %fusion.21), channel_id=1, replica_groups=mesh['light'=64,'tex'=4] {'light'}, dimensions={0}, use_global_device_ids=true | all-gather | bytes 133120 | tf_op jit(solution)/shard_map/all_gather | solution.py:74
  142.0 3.1 fusion
  145.5 86.7 %all_to_all.40 = bf16[4,128,4608]{2,1,0:T(8,128)(2,1)S(1)} all-to-all(bf16[4,128,4608]{2,1,0:T(8,128)(2,1)S(1)} %stack.2), channel_id=1, replica_groups=mesh['light'=64,'tex'=4] {'tex'}, dimensions={0} | all-to-all | bytes 9437184 | tf_op jit(solution)/shard_map/all_to_all | solution.py:79
  232.2 5.8 copy.15
  238.0 11.8 %all_to_all.30 = bf16[64,2,18432]{2,1,0:T(2,128)(2,1)} reshape(bf16[128,4,4608]{2,1,0:T(4,128)(2,1)} %copy.15) | data formatting | bytes 9437184 | tf_op jit(solution)/shard_map/all_to_all | solution.py:81
  249.8 5.8 all-to-all-start.1
  255.7 2.9 collective-permute-start
  258.6 2.4 collective-permute-start.1
  261.1 5.6 collective-permute-done
  266.7 1.8 collective-permute-done.1
  269.0 1.0 slice_dynamic-update-slice_fusion.23
  270.0 1.0 fusion.18
  271.0 1.3 slice_dynamic-update-slice_fusion.22
  272.3 1.0 slice_dynamic-update-slice_fusion.21
  273.4 1.1 constant_dynamic-update-slice_fusion
  274.4 1.3 slice_dynamic-update-slice_fusion.20
  275.8 1.0 slice_dynamic-update-slice_fusion.19
  276.7 1.0 fusion.17
  277.7 1.4 slice_dynamic-update-slice_fusion.18
  279.1 78.8 %all-to-all-done.1 = bf16[64,2,18432]{2,1,0:T(2,128)(2,1)} async-done(((bf16[64,2,18432]{2,1,0:T(2,128)(2,1)}), bf16[64,2,18432]{2,1,0:T(2,128)(2,1)}, u32[]{:S(2)}, u32[]{:S(2)}) %all-to-all-start.1) | async-done | bytes 4718624 | tf_op jit(solution)/shard_map/all_to_all | solution.py:81
  357.8 5.5 fusion.25
  363.4 8.0 %multiply_convert_fusion.4 = (bf16[2,16,48,256]{3,2,1,0:T(8,128)(2,1)S(1)}, f32[2,16,48,256]{3,2,1,0:T(8,128)}) fusion(bf16[2,16,48,2304]{3,2,1,0:T(8,128)(2,1)} %slice_dynamic-update-slice_fusion.18, bf16[1,2,2304,256]{3,1,2,0:T(2,128)(2,1)S(1)} %bitcast.82), kind=kOutput, calls=%fused_computation.19 | convolution fusion | flops 1813905408 | bytes 11796480 | tf_op jit(solution)/shard_map/lrck,lko->lrco/dot_general | solution.py:56
  371.4 8.9 %collective-permute-start.2 = (bf16[2,1,48,256]{3,2,1,0:T(8,128)(2,1)S(1)}, bf16[2,1,48,256]{3,2,1,0:T(8,128)(2,1)S(1)}, u32[]{:S(2)}, u32[]{:S(2)}) collective-permute-start(bf16[2,1,48,256]{3,2,1,0:T(8,128)(2,1)S(1)} %get-tuple-element.11), channel_id=1, source_target_pairs={{0,1},{1,2},{2,3},{4,5},{5,6},{6,7},{8,9},{9,10},{10,11},{12,13},{... | collective-permute-start | bytes 147464 | tf_op jit(solution)/shard_map/ppermute | solution.py:13
  380.3 1.9 collective-permute-start.3
  382.2 1.7 copy.27
  383.9 2.8 copy.16
  386.8 1.6 rev.6
  391.3 3.4 multiply_convert_fusion.2
  394.7 5.2 collective-permute-start.4
  399.9 1.9 collective-permute-start.5
  401.8 4.4 fusion.2
  406.2 3.2 concatenate.78
  409.4 3.8 copy.19
  416.4 2.3 multiply_convert_fusion.1
  418.7 7.3 %fusion.1 = bf16[2,2304,256]{2,1,0:T(8,128)(2,1)} fusion(bf16[2,16,48,2304]{3,2,1,0:T(8,128)(2,1)} %slice_dynamic-update-slice_fusion.18, bf16[2,16,48,256]{3,2,1,0:T(8,128)(2,1)S(1)} %multiply_convert_fusion.1), kind=kOutput, calls=%fused_computation.6 | convolution fusion | flops 1813118976 | bytes 10223616 | tf_op jit(solution)/shard_map/lrck,lrco->lko/dot_general | solution.py:60
  426.0 3.2 concatenate.77
  429.2 3.9 copy.18
  433.1 10.6 %pad_maximum_fusion = bf16[2,64,18432]{2,0,1:T(2,128)(2,1)} fusion(bf16[2,32,18432]{2,0,1:T(2,128)(2,1)} %copy.19, bf16[2,32,18432]{2,0,1:T(2,128)(2,1)} %copy.18), kind=kLoop, calls=%fused_computation.5 | loop fusion | flops 2359296 | bytes 9437184 | tf_op jit(solution)/shard_map/concatenate | solution.py:102
  443.7 111.8 %all_to_all.41 = bf16[2,64,18432]{2,0,1:T(2,128)(2,1)} all-to-all(bf16[2,64,18432]{2,0,1:T(2,128)(2,1)} %pad_maximum_fusion), channel_id=1, replica_groups=mesh['light'=64,'tex'=4] {'light'}, dimensions={1} | all-to-all | bytes 9437184 | tf_op jit(solution)/shard_map/all_to_all | solution.py:105
  555.6 7.5 %all_to_all.36 = bf16[128,18432]{1,0:T(8,128)(2,1)} reshape(bf16[64,2,18432]{2,1,0:T(2,128)(2,1)} %bitcast.79) | data formatting | bytes 9437184 | tf_op jit(solution)/shard_map/all_to_all | solution.py:105
  563.1 5.4 collective-permute-start.6
  568.5 1.9 collective-permute-start.7
  570.5 2.0 copy.26
  572.5 2.7 copy.17
  575.2 1.9 rev.7
  579.3 2.9 convolution_convert_fusion
  582.2 37.0 %reduce-scatter.2.cloned.1.call-done = bf16[128,4608]{1,0:T(8,128)(2,1)} async-done(((bf16[128,18432]{1,0:T(8,128)(2,1)}), bf16[128,4608]{1,0:T(8,128)(2,1)}) %reduce-scatter.2.cloned.1.call-update) | async-done | bytes 1179664 | tf_op jit(solution)/shard_map/reduce_scatter | solution.py:108
  619.2 4.9 multiply_convert_fusion
  (69 shorter events, 11.2 us)
Async XLA Ops:
  7.2 1.0 copy-start
  249.8 5.9 copy-start.2
  249.8 108.1 %all-to-all-start.1 = ((bf16[64,2,18432]{2,1,0:T(2,128)(2,1)}), bf16[64,2,18432]{2,1,0:T(2,128)(2,1)}, u32[]{:S(2)}, u32[]{:S(2)}) async-start(bf16[64,2,18432]{2,1,0:T(2,128)(2,1)} %all_to_all.30), calls=%async_computation.1 | async-start | bytes 9437184 | tf_op jit(solution)/shard_map/all_to_all | solution.py:81
  255.6 363.6 %reduce-scatter.2.cloned.1.call-start = ((), (), s32[]{:S(2)}) async-start(), calls=%async_computation.4 | async-start | bytes 5898240 | tf_op jit(solution)/shard_map/reduce_scatter | solution.py:108
  255.7 11.0 %collective-permute-start = (bf16[2,1,48,256]{3,2,1,0:T(8,128)(2,1)S(1)}, bf16[2,1,48,256]{3,2,1,0:T(8,128)(2,1)S(1)}, u32[]{:S(2)}, u32[]{:S(2)}) collective-permute-start(bf16[2,1,48,256]{3,2,1,0:T(8,128)(2,1)S(1)} %get-tuple-element.13), channel_id=1, source_target_pairs={{0,1},{1,2},{2,3},{4,5},{5,6},{6,7},{8,9},{9,10},{10,11},{12,13},{... | collective-permute-start | bytes 147464 | tf_op jit(solution)/shard_map/ppermute | solution.py:13
  258.6 9.8 %collective-permute-start.1 = (bf16[2,1,48,256]{3,2,1,0:T(8,128)(2,1)S(1)}, bf16[2,1,48,256]{3,2,1,0:T(8,128)(2,1)S(1)}, u32[]{:S(2)}, u32[]{:S(2)}) collective-permute-start(bf16[2,1,48,256]{3,2,1,0:T(8,128)(2,1)S(1)} %get-tuple-element.14), channel_id=1, source_target_pairs={{1,0},{2,1},{3,2},{5,4},{6,5},{7,6},{9,8},{10,9},{11,10},{13,12},{... | collective-permute-start | bytes 147464 | tf_op jit(solution)/shard_map/ppermute | solution.py:16
  363.4 8.1 %copy-start.3 = (bf16[2,589824]{1,0:T(2,128)(2,1)}, bf16[2,589824]{1,0:T(2,128)(2,1)S(1)}, u32[]{:S(2)}) copy-start(bf16[2,589824]{1,0:T(2,128)(2,1)S(1)} %get-tuple-element.4) | copy-start | bytes 7077892
  363.4 18.9 %copy-start.4 = (bf16[2,589824]{1,0:T(2,128)(2,1)}, bf16[2,589824]{1,0:T(2,128)(2,1)S(1)}, u32[]{:S(2)}) copy-start(bf16[2,589824]{1,0:T(2,128)(2,1)S(1)} %get-tuple-element.3) | copy-start | bytes 7077892
  371.4 16.9 %collective-permute-start.2 = (bf16[2,1,48,256]{3,2,1,0:T(8,128)(2,1)S(1)}, bf16[2,1,48,256]{3,2,1,0:T(8,128)(2,1)S(1)}, u32[]{:S(2)}, u32[]{:S(2)}) collective-permute-start(bf16[2,1,48,256]{3,2,1,0:T(8,128)(2,1)S(1)} %get-tuple-element.11), channel_id=1, source_target_pairs={{0,1},{1,2},{2,3},{4,5},{5,6},{6,7},{8,9},{9,10},{10,11},{12,13},{... | collective-permute-start | bytes 147464 | tf_op jit(solution)/shard_map/ppermute | solution.py:13
  380.3 8.1 %collective-permute-start.3 = (bf16[2,1,48,256]{3,2,1,0:T(8,128)(2,1)S(1)}, bf16[2,1,48,256]{3,2,1,0:T(8,128)(2,1)S(1)}, u32[]{:S(2)}, u32[]{:S(2)}) collective-permute-start(bf16[2,1,48,256]{3,2,1,0:T(8,128)(2,1)S(1)} %get-tuple-element.12), channel_id=1, source_target_pairs={{1,0},{2,1},{3,2},{5,4},{6,5},{7,6},{9,8},{10,9},{11,10},{13,12},{... | collective-permute-start | bytes 147464 | tf_op jit(solution)/shard_map/ppermute | solution.py:16
  389.5 1.7 copy-start.5
  389.5 1.8 copy-start.7
  394.7 18.5 %collective-permute-start.4 = (bf16[2,1,48,256]{3,2,1,0:T(8,128)(2,1)S(1)}, bf16[2,1,48,256]{3,2,1,0:T(8,128)(2,1)S(1)}, u32[]{:S(2)}, u32[]{:S(2)}) collective-permute-start(bf16[2,1,48,256]{3,2,1,0:T(8,128)(2,1)S(1)} %get-tuple-element.9), channel_id=1, source_target_pairs={{0,1},{1,2},{2,3},{4,5},{5,6},{6,7},{8,9},{9,10},{10,11},{12,13},{... | collective-permute-start | bytes 147464 | tf_op jit(solution)/shard_map/ppermute | solution.py:13
  399.9 13.3 %collective-permute-start.5 = (bf16[2,1,48,256]{3,2,1,0:T(8,128)(2,1)S(1)}, bf16[2,1,48,256]{3,2,1,0:T(8,128)(2,1)S(1)}, u32[]{:S(2)}, u32[]{:S(2)}) collective-permute-start(bf16[2,1,48,256]{3,2,1,0:T(8,128)(2,1)S(1)} %get-tuple-element.10), channel_id=1, source_target_pairs={{1,0},{2,1},{3,2},{5,4},{6,5},{7,6},{9,8},{10,9},{11,10},{13,12},{... | collective-permute-start | bytes 147464 | tf_op jit(solution)/shard_map/ppermute | solution.py:16
  414.3 1.7 copy-start.6
  414.3 2.1 copy-start.8
  563.1 14.0 %collective-permute-start.6 = (bf16[2,1,48,256]{3,2,1,0:T(8,128)(2,1)S(1)}, bf16[2,1,48,256]{3,2,1,0:T(8,128)(2,1)S(1)}, u32[]{:S(2)}, u32[]{:S(2)}) collective-permute-start(bf16[2,1,48,256]{3,2,1,0:T(8,128)(2,1)S(1)} %get-tuple-element.7), channel_id=1, source_target_pairs={{0,1},{1,2},{2,3},{4,5},{5,6},{6,7},{8,9},{9,10},{10,11},{12,13},{... | collective-permute-start | bytes 147464 | tf_op jit(solution)/shard_map/ppermute | solution.py:13
  568.5 8.6 %collective-permute-start.7 = (bf16[2,1,48,256]{3,2,1,0:T(8,128)(2,1)S(1)}, bf16[2,1,48,256]{3,2,1,0:T(8,128)(2,1)S(1)}, u32[]{:S(2)}, u32[]{:S(2)}) collective-permute-start(bf16[2,1,48,256]{3,2,1,0:T(8,128)(2,1)S(1)} %get-tuple-element.8), channel_id=1, source_target_pairs={{1,0},{2,1},{3,2},{5,4},{6,5},{7,6},{9,8},{10,9},{11,10},{13,12},{... | collective-permute-start | bytes 147464 | tf_op jit(solution)/shard_map/ppermute | solution.py:16
  579.3 44.8 %copy-start.1 = (bf16[256,512]{1,0:T(8,128)(2,1)S(1)}, bf16[256,512]{1,0:T(8,128)(2,1)}, u32[]{:S(2)}) copy-start(bf16[256,512]{1,0:T(8,128)(2,1)} %param.8) | copy-start | bytes 786436
Sparse Core Ops, SparseCore 0:
  563.2 55.9 reduce-scatter.1
